TPU v7x, 32 devices: a whole 2x2x4 slice. The times are simulated.
32 devices in a mesh: tm: 4 (over y, core), fiber: 8 (over z, x).
Axes of the slice: x: 2, y: 2, z: 4, core: 2. Of those that a mesh axis runs over, the one named last changes fastest.
Arguments:
- waveform: bfloat16 [4096, 8192], P('fiber', 'tm'), may hold values from -6 to 6
- filters: bfloat16 [512, 256], replicated, may hold values from -0.25 to 0.25
- channel_section: int32 [4096], replicated, may hold values from 0 to 127, never falling along the last dimension, each value on 1 to 64 neighbouring positions
- section_bank: int32 [128, 8], replicated, may hold values from 0 to 1
- conv_bank: bfloat16 [2, 8, 3, 3, 32, 32], P(None, 'fiber'), may hold values from -0.375 to 0.375
Outputs:
- events: bfloat16 [4096, 256, 64], P('tm', 'fiber')
Inputs may be any that keep to these rules, and one draw needn't show every extreme that they name: `channel_section`: never falls along the channels; every section has 1 to 64 channels.
All inputs are finite; a program needn't handle non-finite values.
Results may differ from a plain program's by a relative error of at most 0.005.
Values may be sent and summed in bfloat16 or wider, within the bound.
A program may use at most 128 MiB of HBM per device.

v0:
```python
import math

import jax
import jax.numpy as jnp
from jax import lax
from jax.sharding import PartitionSpec as P

HOP = 128
GW = 32


def from_behind(block, axis, distance):
    devices = range(lax.axis_size(axis))
    route = [(i - distance, i) for i in devices if i - distance in devices]
    return lax.ppermute(block, axis, route)


def extended_2(x, sides, width):
    for axis, dim in sides:
        size, length = (lax.axis_size(axis), x.shape[dim])
        up = [(i, (i + 1) % size) for i in range(size - 1)]
        down = [(j, i) for i, j in up]
        last = lax.slice_in_dim(x, length - width, length, axis=dim)
        first = lax.slice_in_dim(x, 0, width, axis=dim)
        before = lax.ppermute(last, axis, up)
        after = lax.ppermute(first, axis, down)
        x = jnp.concatenate([before, x, after], axis=dim)
    return x


def shards(waveform, filters, channel_section, section_bank, conv_bank):
    ch_dev, samp_dev = waveform.shape
    taps, nfilt = filters.shape
    frames_dev = samp_dev // HOP
    groups = nfilt // GW
    rim = from_behind(waveform[:, : taps - HOP], "tm", -1)
    extended = jnp.concatenate([waveform, rim], axis=1)
    blocks = extended.reshape(ch_dev, frames_dev + taps // HOP - 1, HOP)
    banded = filters.reshape(taps, groups, GW)
    total = jnp.zeros((ch_dev, groups, frames_dev, GW), jnp.float32)
    for k in range(taps // HOP):
        total = total + jnp.einsum(
            "cfh,hgw->cgfw",
            blocks[:, k : k + frames_dev],
            banded[k * HOP : (k + 1) * HOP],
            preferred_element_type=jnp.float32,
        )
    features = total.astype(jnp.bfloat16).reshape(ch_dev, groups, frames_dev * GW)
    tm_count = lax.axis_size("tm")
    fiber_count = lax.axis_size("fiber")
    rows = ch_dev * fiber_count // tm_count
    local_groups = groups // fiber_count
    by_band = lax.all_to_all(features, "fiber", split_axis=1, concat_axis=0, tiled=True)
    owned = lax.all_to_all(by_band, "tm", split_axis=0, concat_axis=2, tiled=True)
    framed = extended_2(owned, (("tm", 0),), 1)
    frames = framed.shape[2] // GW
    planes = framed.reshape(rows + 2, local_groups, frames, GW).transpose(0, 1, 3, 2)
    planes = jnp.pad(planes, ((0, 0), (0, 0), (0, 0), (1, 1)))
    start_row = lax.axis_index("tm") * rows
    edge = jnp.array([-1], jnp.int32)
    sec_all = jnp.concatenate([edge, channel_section, edge])
    sec = lax.dynamic_slice_in_dim(sec_all, start_row, rows + 2, 0)
    same_lo = (sec[:-2] == sec[1:-1]).astype(jnp.bfloat16)
    same_hi = (sec[2:] == sec[1:-1]).astype(jnp.bfloat16)
    middle_sec = sec[1:-1]
    table = lax.dynamic_slice_in_dim(
        section_bank, lax.axis_index("fiber") * local_groups, local_groups, 1
    )
    onehot = (middle_sec[:, None] == jnp.arange(table.shape[0], dtype=jnp.int32)[None, :]).astype(
        jnp.int32
    )
    choose = jnp.dot(onehot, table)
    banks = conv_bank.shape[0]
    pick_all = (choose[:, :, None] == jnp.arange(banks, dtype=jnp.int32)[None, None, :]).astype(
        jnp.float32
    )
    block = math.gcd(rows, 32)
    count = rows // block

    def conv_rows(start):
        xs = lax.dynamic_slice_in_dim(planes, start, block + 2, 0)
        low = lax.dynamic_slice_in_dim(same_lo, start, block, 0)
        high = lax.dynamic_slice_in_dim(same_hi, start, block, 0)
        pick = lax.dynamic_slice_in_dim(pick_all, start, block, 0)
        acc = jnp.zeros((block, local_groups, banks, GW, frames), jnp.float32)
        for d in range(3):
            part = xs[d : d + block]
            if d == 0:
                part = part * low[:, None, None, None]
            if d == 2:
                part = part * high[:, None, None, None]
            for e in range(3):
                acc = acc + jnp.einsum(
                    "bgoi,cgit->cgbot",
                    conv_bank[:, :, d, e],
                    part[..., e : e + frames],
                    preferred_element_type=jnp.float32,
                )
        out = jnp.sum(acc * pick[:, :, :, None, None], axis=2)
        return out.astype(jnp.bfloat16).reshape(block, local_groups * GW, frames)

    starts = jnp.arange(count, dtype=jnp.int32) * block
    result = lax.map(conv_rows, starts)
    return result.reshape(rows, local_groups * GW, frames)


def solution(mesh):
    placed = (P("fiber", "tm"), P(), P(), P(), P(None, "fiber", None, None, None, None))
    return jax.shard_map(
        shards, mesh=mesh, in_specs=placed, out_specs=P("tm", "fiber", None), check_vma=False
    )
```

profile of v0, /device:TPU:1, one launch (start us, length us, event | category | flops | bytes accessed | tf_op | source)
XLA Modules:
  0.0 654.2 jit_solution(14298002486186150269)
XLA Ops:
  0.0 2.9 copy.35
  3.0 2.0 collective-permute-start
  5.4 7.5 %collective-permute-done = bf16[512,384]{0,1:T(8,128)(2,1)S(1)} collective-permute-done((bf16[512,384]{0,1:T(8,128)(2,1)S(1)}, bf16[512,384]{0,1:T(8,128)(2,1)S(1)}, u32[]{:S(2)}, u32[]{:S(2)}) %collective-permute-start) | collective-permute-done | bytes 393248 | tf_op jit(solution)/shard_map/ppermute | solution.py:15
  14.4 4.5 fusion.28
  19.0 4.5 fusion.29
  23.5 8.7 %fusion.26 = bf16[512,8,16,32]{0,3,1,2:T(8,128)(2,1)} fusion(f32[512,16,8,32]{0,3,2,1:T(8,128)S(1)} %fusion.27, f32[512,16,8,32]{0,3,2,1:T(8,128)} %fusion.29, f32[512,16,8,32]{0,3,2,1:T(8,128)} %fusion.28, bf16[128,8,32,1]{0,2,1,3:T(8,128)(2,1)S(1)} %bitcast.229, bf16[512,19,128]{0,2,1:T(8,128)(2,1)S(1)} %bitcast.217), kind=kOutput, calls=%fused_computation.48 | convolution fusion | flops 545259520 | bytes 31522816 | tf_op jit(solution)/shard_map/cfh,hgw->cgfw/dot_general | solution.py:42
  32.2 2.7 copy.44
  34.9 94.8 %all_to_all.33 = bf16[512,8,512]{0,2,1:T(8,128)(2,1)} all-to-all(bf16[512,8,512]{0,2,1:T(8,128)(2,1)S(1)} %bitcast.223), channel_id=1, replica_groups=mesh['tm'=4,'fiber'=8] {'fiber'}, dimensions={1} | all-to-all | bytes 8388608 | tf_op jit(solution)/shard_map/all_to_all | solution.py:53
  129.7 6.4 copy.45
  136.7 6.7 %reduce.5 = bf16[4096,512]{1,0:T(8,128)(2,1)} reduce(bf16[4096,1,512]{2,0,1:T(8,128)(2,1)} %bitcast.222, bf16[]{:T(256)} %broadcast.33), dimensions={1}, to_apply=%copy.46.reduce_sub_computation | reduce | bytes 8388610 | tf_op jit(solution)/shard_map/all_to_all | solution.py:53
  143.3 6.2 reshape.199
  149.6 4.9 all-to-all-start.1
  155.3 44.3 %all-to-all-done.1 = bf16[4,2,262144]{2,1,0:T(2,128)(2,1)} async-done(((bf16[4,2,262144]{2,1,0:T(2,128)(2,1)}), bf16[4,2,262144]{2,1,0:T(2,128)(2,1)}, u32[]{:S(2)}, u32[]{:S(2)}) %all-to-all-start.1) | async-done | bytes 4194336 | tf_op jit(solution)/shard_map/all_to_all | solution.py:54
  199.6 7.4 %reshape.200 = bf16[4096,1,512]{2,1,0:T(2,128)(2,1)} reshape(bf16[4,2,262144]{2,1,0:T(2,128)(2,1)} %all-to-all-done.1) | data formatting | bytes 8388608
  207.0 4.7 copy.66
  211.7 2.0 copy-done.2
  213.7 2.7 collective-permute-start.1
  216.4 2.3 collective-permute-start.2
  218.8 6.3 copy.47
  227.2 9.4 %concatenate.20 = bf16[1026,1,64,32]{0,3,2,1:T(8,128)(2,1)} concatenate(bf16[1,1,64,32]{0,3,2,1:T(8,128)(2,1)S(1)} %concatenate.22, bf16[1024,1,64,32]{0,3,2,1:T(8,128)(2,1)} %bitcast.221, bf16[1,1,64,32]{0,3,2,1:T(8,128)(2,1)S(1)} %concatenate.23), dimensions={0} | concatenate | bytes 8404992 | tf_op jit(solution)/shard_map/concatenate | solution.py:27
  236.6 16.9 %copy.71 = bf16[1026,1,32,64]{3,2,0,1:T(8,128)(2,1)} copy(bf16[1026,1,32,64]{0,2,3,1:T(8,128)(2,1)} %bitcast.218) | data formatting | bytes 8404992
  253.4 8.3 %pad.4.clone = bf16[1026,1,32,66]{3,2,0,1:T(8,128)(2,1)} pad(bf16[1026,1,32,64]{3,2,0,1:T(8,128)(2,1)} %copy.71, bf16[]{:T(256)} %constant.22.clone.1), padding=0_0x0_0x0_0x1_1 | pad | bytes 8536322 | tf_op jit(solution)/shard_map/jit(_pad)/pad | solution.py:58
  261.7 382.8 %while.10 = (s32[]{:T(128)}, bf16[32,32,32,64]{3,2,1,0:T(8,128)(2,1)}, s32[32]{0:T(128)S(1)}, bf16[1026,1,32,66]{3,2,0,1:T(8,128)(2,1)}, bf16[1024]{0:T(1024)(12...) while((s32[]{:T(128)}, ...), condition=%wide.region_2.3_spmd, body=%wide.region_0.2_spmd.sunk | while | flops 76877832 | bytes 16173220 | solution.py:103
  644.5 9.8 %copy.52 = bf16[1024,32,64]{0,2,1:T(8,128)(2,1)} copy(bf16[1024,32,64]{2,1,0:T(8,128)(2,1)} %bitcast.225) | data formatting | bytes 8388608 | tf_op jit(solution)/shard_map/reshape | solution.py:104
  (547 shorter events, 281.7 us)
Async XLA Ops:
  0.0 154.8 %copy-start = (s32[128,8]{0,1:T(8,128)S(1)}, s32[128,8]{0,1:T(8,128)}, u32[]{:S(2)}) copy-start(s32[128,8]{0,1:T(8,128)} %param.11) | copy-start | bytes 12292
  0.0 4.9 copy-start.3
  3.0 10.0 %collective-permute-start = (bf16[512,384]{0,1:T(8,128)(2,1)S(1)}, bf16[512,384]{0,1:T(8,128)(2,1)S(1)}, u32[]{:S(2)}, u32[]{:S(2)}) collective-permute-start(bf16[512,384]{0,1:T(8,128)(2,1)S(1)} %slice.152), channel_id=1, source_target_pairs={{8,0},{16,8},{24,16},{9,1},{17,9},{25,17},{10,2},{18,10},{26,18},{... | collective-permute-start | bytes 1179656 | tf_op jit(solution)/shard_map/ppermute | solution.py:15
  149.6 5.0 copy-start.5
  149.6 50.0 %all-to-all-start.1 = ((bf16[4,2,262144]{2,1,0:T(2,128)(2,1)}), bf16[4,2,262144]{2,1,0:T(2,128)(2,1)}, u32[]{:S(2)}, u32[]{:S(2)}) async-start(bf16[4,2,262144]{2,1,0:T(2,128)(2,1)} %reshape.199), calls=%async_computation.1 | async-start | bytes 8388608 | tf_op jit(solution)/shard_map/all_to_all | solution.py:54
  207.0 11.7 %copy-start.4 = (bf16[2,1,3,3,32,32]{5,4,3,2,1,0:T(8,128)(2,1)S(1)}, bf16[2,1,3,3,32,32]{5,4,3,2,1,0:T(8,128)(2,1)}, u32[]{:S(2)}) copy-start(bf16[2,1,3,3,32,32]{5,4,3,2,1,0:T(8,128)(2,1)} %param.12) | copy-start | bytes 110596
  211.7 2.0 copy-start.2
  213.7 11.4 %collective-permute-start.1 = (bf16[1,1,2048]{2,1,0:T(2,128)(2,1)S(1)}, bf16[1,1,2048]{2,1,0:T(2,128)(2,1)S(1)}, u32[]{:S(2)}, u32[]{:S(2)}) collective-permute-start(bf16[1,1,2048]{2,1,0:T(2,128)(2,1)S(1)} %bitcast.231), channel_id=1, source_target_pairs={{0,8},{8,16},{16,24},{1,9},{9,17},{17,25},{2,10},{10,18},{18,26},{... | collective-permute-start | bytes 12296 | tf_op jit(solution)/shard_map/ppermute | solution.py:25
  216.4 9.7 %collective-permute-start.2 = (bf16[1,1,2048]{2,1,0:T(2,128)(2,1)S(1)}, bf16[1,1,2048]{2,1,0:T(2,128)(2,1)S(1)}, u32[]{:S(2)}, u32[]{:S(2)}) collective-permute-start(bf16[1,1,2048]{2,1,0:T(2,128)(2,1)S(1)} %bitcast.230), channel_id=1, source_target_pairs={{8,0},{16,8},{24,16},{9,1},{17,9},{25,17},{10,2},{18,10},{26,18},{... | collective-permute-start | bytes 12296 | tf_op jit(solution)/shard_map/ppermute | solution.py:26
  644.5 9.8 %copy-start.1 = (s32[128,8]{0,1:T(8,128)S(1)}, s32[128,8]{0,1:T(8,128)}, u32[]{:S(2)}) copy-start(s32[128,8]{0,1:T(8,128)} %param.11) | copy-start | bytes 12292
where the time goes:
time: 661 us; the launch traced here: 654 us
  matrix products  206 us (31%)
  local copies, waits for them, and re-layouts  138 us (21%)
  loops' own time  107 us (16%)
  blocking collectives  94.8 us (14%)
  waiting for transfers between devices  51.8 us (8%)
  other arithmetic  44.5 us (7%)
  starting transfers between devices  11.9 us (2%)
    dot_general x288, matrix products, conv_rows(): jnp.einsum('bgoi,cgit->cgbot', conv_bank[:, :, d, e], part[..., e:e + fra...  187 us
    another operation x1, loops' own time, shards(): result = lax.map(conv_rows, starts)  107 us
    all_to_all x1, blocking collectives, shards(): lax.all_to_all(features, 'fiber', split_axis=1, concat_axis=0, tiled=True)  94.8 us
    all_to_all x1, waiting for transfers between devices, shards(): lax.all_to_all(by_band, 'tm', split_axis=0, concat_axis=2, tiled=True)  44.3 us
    unnamed x17, local copies, waits for them, and re-layouts  40.1 us
    mul x32, other arithmetic, conv_rows(): part = part * high[:, None, None, None]  37.4 us
    dynamic_update_slice x32, local copies, waits for them, and re-layouts, shards(): result = lax.map(conv_rows, starts)  23.2 us
    dot_general x4, matrix products, shards(): jnp.einsum('cfh,hgw->cgfw', blocks[:, k:k + frames_dev], banded[k * HOP:(...  19.1 us
  transfers between devices with their start and end apart: 4, of which 2 were waited for; matrix products, arithmetic and copies ran while one was open for 1% of the time, Pallas kernels for 0%

commit v1 on v0

v1 whole, which is shorter than its diff:
```python
import functools

import jax
import jax.numpy as jnp
from jax import lax
from jax.experimental import pallas as pl
from jax.experimental.pallas import tpu as pltpu
from jax.sharding import PartitionSpec as P

HOP = 128
GW = 32
LANES = 128
MESH = pl.DeviceIdType.MESH
NT_DIMS = (((1,), (1,)), ((), ()))


def kernel(nt, nf, wave, filt_t, bands, section, table, out, w, ft, s, r1, x, marks,
           load_sem, rim_sem, s1_send, s1_recv, s2_send, x_recv, h_send, h_recv):
    t = lax.axis_index("tm")
    f = lax.axis_index("fiber")
    ch_dev, samp = wave.shape
    rim = w.shape[1] - samp
    span = ft.shape[1]
    hops = (span - rim) // HOP
    blk = hops * GW
    nb = samp // (HOP * hops)
    rows = out.shape[2]
    q = min(rows, ch_dev)
    ndc, nsub = rows // q, ch_dev // q
    part = nb * blk
    half = nf // 2

    load = pltpu.make_async_copy(wave, w.at[:, pl.ds(0, samp)], load_sem)
    load.start()

    barrier = pltpu.get_barrier_semaphore()
    for k in range(1, nf):
        pl.semaphore_signal(barrier, inc=1, device_id=(t, f ^ k), device_id_type=MESH)
    for j in range(1, nt):
        pl.semaphore_signal(barrier, inc=1, device_id=(lax.rem(t + j, nt), f), device_id_type=MESH)
    pl.semaphore_wait(barrier, nf - 1 + nt - 1)

    def rim_copy(to):
        return pltpu.make_async_remote_copy(
            src_ref=wave.at[:, pl.ds(0, rim)], dst_ref=w.at[:, pl.ds(samp, rim)],
            send_sem=rim_sem.at[0], recv_sem=rim_sem.at[1],
            device_id=(to, f), device_id_type=MESH)

    @pl.when(t > 0)
    def _():
        rim_copy(t - 1).start()

    @pl.when(t == nt - 1)
    def _():
        w[:, samp:] = jnp.zeros((ch_dev, rim), w.dtype)

    taps = filt_t.shape[1]
    ft[...] = jnp.zeros(ft.shape, ft.dtype)
    for g in range(nf):
        for h in range(hops):
            ft[g * blk + h * GW:g * blk + (h + 1) * GW, h * HOP:h * HOP + taps] = (
                filt_t[g * GW:(g + 1) * GW, :])
    load.wait()

    def rowsof(g, b):
        return s.at[g, pl.ds(b * blk, blk), :]

    def first(k, b):
        g = f ^ k
        return pltpu.make_async_remote_copy(
            src_ref=rowsof(g, b), dst_ref=r1.at[f, pl.ds(b * blk, blk), :],
            send_sem=s1_send.at[k, b], recv_sem=s1_recv.at[k, b],
            device_id=(t, g), device_id_type=MESH)

    def features(b, side):
        lo = pl.multiple_of(side * (half * blk), half * blk)
        res = lax.dot_general(
            ft[pl.ds(lo, half * blk), :], w[:, b * hops * HOP:b * hops * HOP + span], NT_DIMS,
            preferred_element_type=jnp.float32).astype(s.dtype)
        for g in range(half):
            s[side * half + g, b * blk:(b + 1) * blk, :] = res[g * blk:(g + 1) * blk]

    mine = f // half
    for b in range(nb):
        if b == nb - 1:
            @pl.when(t < nt - 1)
            def _():
                rim_copy(t).wait_recv()
        features(b, 1 - mine)
        for k in range(nf - 1, half - 1, -1):
            first(k, b).start()
    for b in range(nb):
        features(b, mine)
        for k in range(half - 1, 0, -1):
            first(k, b).start()

    chans = section.shape[1]
    sec = section[...]
    lane = lax.broadcasted_iota(jnp.int32, (1, chans), 1)
    low = jnp.logical_and(pltpu.roll(sec, 1, 1) == sec, lane > 0)
    high = jnp.logical_and(pltpu.roll(sec, chans - 1, 1) == sec, lane < chans - 1)
    marks[0:1, :] = low.astype(jnp.float32)
    marks[1:2, :] = high.astype(jnp.float32)
    tab = table[...]
    here = lax.broadcasted_iota(jnp.int32, tab.shape, 0) == f
    column = jnp.sum(jnp.where(here, tab, 0).astype(jnp.float32), axis=0, keepdims=True)
    wide = min(chans, 512)
    for c in range(0, chans, wide):
        hot = lax.broadcasted_iota(jnp.int32, (tab.shape[1], wide), 0) == sec[:, c:c + wide]
        marks[2:3, c:c + wide] = jnp.dot(
            column, hot.astype(jnp.float32), preferred_element_type=jnp.float32)
    total = x.shape[0]
    x[0:GW, :] = jnp.zeros((GW, x.shape[1]), x.dtype)
    x[total - GW:total, :] = jnp.zeros((GW, x.shape[1]), x.dtype)

    @pl.when(t == 0)
    def _():
        x[GW:total - GW, 0:LANES] = jnp.zeros((total - 2 * GW, LANES), x.dtype)

    @pl.when(t == nt - 1)
    def _():
        x[GW:total - GW, LANES + rows:] = jnp.zeros((total - 2 * GW, LANES), x.dtype)

    def place(source_t, slot, b):
        return x.at[pl.ds(GW + source_t * part + b * blk, blk), pl.ds(LANES + slot * q, q)]

    def second(k, b, i):
        fb = f ^ k
        gc = fb * nsub + i
        to = gc // ndc
        slot = gc % ndc
        src = (s if k == 0 else r1).at[fb, pl.ds(b * blk, blk), pl.ds(i * q, q)]
        dst = place(t, slot, b)
        sem = x_recv.at[t, slot, b]
        return to, pltpu.make_async_copy(src, dst, sem), pltpu.make_async_remote_copy(
            src_ref=src, dst_ref=dst, send_sem=s2_send.at[k, b, i], recv_sem=sem,
            device_id=(to, f), device_id_type=MESH)

    def halo(k, i, upper):
        fb = f ^ k
        gc = fb * nsub + i
        owner = gc // ndc
        to = owner + 1 if upper else owner - 1
        edge = lax.rem(gc, ndc) == (ndc - 1 if upper else 0)
        there = jnp.logical_and(edge, jnp.logical_and(to >= 0, to < nt))
        column = (i + 1) * q - LANES if upper else i * q
        src = (s if k == 0 else r1).at[fb, :, pl.ds(column, LANES)]
        dst = x.at[pl.ds(GW + t * part, part), pl.ds(0 if upper else LANES + rows, LANES)]
        sem = h_recv.at[t, 0 if upper else 1]
        return there, to, pltpu.make_async_copy(src, dst, sem), pltpu.make_async_remote_copy(
            src_ref=src, dst_ref=dst, send_sem=h_send.at[k, i, 0 if upper else 1], recv_sem=sem,
            device_id=(to, f), device_id_type=MESH)

    order = list(range(nf - 1, half - 1, -1)), list(range(half - 1, -1, -1))
    for ks in order:
        for b in range(nb):
            for k in ks:
                if k > 0:
                    first(k, b).wait_recv()
                for i in range(nsub):
                    to, local, remote = second(k, b, i)

                    @pl.when(to == t)
                    def _():
                        local.start()

                    @pl.when(to != t)
                    def _():
                        remote.start()

                    if b == nb - 1:
                        for upper in (True, False):
                            there, to, local, remote = halo(k, i, upper)

                            @pl.when(jnp.logical_and(there, to == t))
                            def _():
                                local.start()

                            @pl.when(jnp.logical_and(there, to != t))
                            def _():
                                remote.start()

    for source in range(nt):
        for slot in range(ndc):
            for b in range(nb):
                ref = place(source, slot, b)
                pltpu.make_async_copy(ref, ref, x_recv.at[source, slot, b]).wait()
        for side, there in ((0, t > 0), (1, t < nt - 1)):
            ref = x.at[pl.ds(GW + source * part, part), pl.ds(side * (LANES + rows), LANES)]

            @pl.when(there)
            def _():
                pltpu.make_async_copy(ref, ref, h_recv.at[source, side]).wait()

    run = 8
    deep = (run + 2) * GW
    lb = min(256, rows)
    ow = out.shape[0]
    pack = 2 * run
    start = t * rows

    def conv(step, carry):
        tt = step // (rows // lb)
        l0 = pl.multiple_of((step % (rows // lb)) * lb, lb)
        here = pl.ds(pl.multiple_of(start + l0, lb), lb)
        low, high, pick = marks[0:1, here], marks[1:2, here], marks[2:3, here]
        both = []
        for h in range(2):
            top = pl.multiple_of(tt * (pack * GW) + h * (run * GW), run * GW)
            block = x[pl.ds(top, deep), pl.ds(l0, lb + 2 * LANES)]
            wide = block.astype(jnp.float32)
            before = pltpu.roll(wide, 1, 1)[:, LANES:LANES + lb] * low
            after = pltpu.roll(wide, lb + 2 * LANES - 1, 1)[:, LANES:LANES + lb] * high
            depth = jnp.concatenate(
                [before.astype(x.dtype), block[:, LANES:LANES + lb], after.astype(x.dtype)], axis=0)
            acc = jnp.dot(bands[...], depth, preferred_element_type=jnp.float32)
            n = acc.shape[0] // 2
            res = acc[:n]
            res = jnp.where(pick == 1.0, acc[n:], res)
            both.append(res.reshape(ow, run, lb))
        out[:, pl.ds(pl.multiple_of(tt * pack, pack), pack), pl.ds(l0, lb)] = (
            jnp.concatenate(both, axis=1).astype(out.dtype))
        return carry

    lax.fori_loop(0, (out.shape[1] // pack) * (rows // lb), conv, 0)

    @pl.when(t > 0)
    def _():
        rim_copy(t - 1).wait_send()

    for k in range(nf):
        for b in range(nb):
            if k > 0:
                first(k, b).wait_send()
            for i in range(nsub):
                to, _, remote = second(k, b, i)

                @pl.when(to != t)
                def _():
                    remote.wait_send()
        for i in range(nsub):
            for upper in (True, False):
                there, to, _, remote = halo(k, i, upper)

                @pl.when(jnp.logical_and(there, to != t))
                def _():
                    remote.wait_send()


def shards(nt, nf, waveform, filters, channel_section, section_bank, conv_bank):
    ch_dev, samp = waveform.shape
    taps, nfilt = filters.shape
    rim = taps - HOP
    hops = LANES // GW
    span = rim + hops * HOP
    nb = samp // (HOP * hops)
    blk = hops * GW
    rows = ch_dev * nf // nt
    frames = samp // HOP * nt
    q = min(rows, ch_dev)
    ndc, nsub = rows // q, ch_dev // q
    banks = conv_bank.shape[0]
    run = 8
    base = conv_bank[:, 0].transpose(0, 3, 1, 2, 4).reshape(banks * GW, 3, 3 * GW)
    bands = jnp.stack(
        [jnp.pad(base, ((0, 0), (0, 0), (r * GW, (run - 1 - r) * GW))) for r in range(run)], axis=1
    ).reshape(banks * GW * run, 3 * (run + 2) * GW)
    dt = waveform.dtype
    vmem = pl.BlockSpec(memory_space=pltpu.VMEM)
    dma = pltpu.SemaphoreType.DMA
    events = pl.pallas_call(
        functools.partial(kernel, nt, nf),
        out_shape=jax.ShapeDtypeStruct((GW, frames, rows), dt),
        in_specs=[pl.BlockSpec(memory_space=pl.ANY)] + [vmem] * 4,
        out_specs=vmem,
        scratch_shapes=[
            pltpu.VMEM((ch_dev, samp + rim), dt),
            pltpu.VMEM((nf * blk, span), dt),
            pltpu.VMEM((nf, nb * blk, ch_dev), dt),
            pltpu.VMEM((nf, nb * blk, ch_dev), dt),
            pltpu.VMEM((frames * GW + 2 * GW, rows + 2 * LANES), dt),
            pltpu.VMEM((8, channel_section.shape[0]), jnp.float32),
            dma, dma((2,)), dma((nf, nb)), dma((nf, nb)), dma((nf, nb, nsub)),
            dma((nt, ndc, nb)), dma((nf, nsub, 2)), dma((nt, 2)),
        ],
        compiler_params=pltpu.CompilerParams(
            collective_id=0, has_side_effects=True, vmem_limit_bytes=56 * 1024 * 1024),
    )(waveform, filters.T, bands, channel_section[None, :], section_bank.T)
    return events.transpose(2, 0, 1)


def solution(mesh):
    placed = (P("fiber", "tm"), P(), P(), P(), P(None, "fiber", None, None, None, None))
    return jax.shard_map(
        functools.partial(shards, mesh.shape["tm"], mesh.shape["fiber"]), mesh=mesh,
        in_specs=placed, out_specs=P("tm", "fiber", None), check_vma=False
    )
```

time: 661 us -> 185 us (0.28)
  matrix products: 206 us -> 0 us
  Pallas kernels: 0 us -> 170 us
  local copies, waits for them, and re-layouts: 138 us -> 12.1 us
  loops' own time: 107 us -> 0 us
  blocking collectives: 94.8 us -> 0 us
  waiting for transfers between devices: 51.8 us -> 0 us
  other arithmetic: 44.5 us -> 0 us
  starting transfers between devices: 11.9 us -> 0 us
    dot_general x293 -> x0, matrix products: 206 us -> none  [the longest x288 187 us: conv_rows(): jnp.einsum('bgoi,cgit->cgbot', conv_bank[:, :, d, e], part[..., e:e + fra...]
    pallas_call x0 -> x1, Pallas kernels: none -> 170 us  [shards(): pl.pallas_call(functools.partial(kernel, nt, nf), out_shape=jax.ShapeDtyp...]
    another operation x1 -> x0, loops' own time: 107 us -> none  [shards(): result = lax.map(conv_rows, starts)]
    all_to_all x1 -> x0, blocking collectives: 94.8 us -> none  [shards(): lax.all_to_all(features, 'fiber', split_axis=1, concat_axis=0, tiled=True)]
    all_to_all x1 -> x0, waiting for transfers between devices: 44.3 us -> none  [shards(): lax.all_to_all(by_band, 'tm', split_axis=0, concat_axis=2, tiled=True)]
    mul x33 -> x0, other arithmetic: 37.4 us -> none  [the longest x32 37.4 us: conv_rows(): part = part * high[:, None, None, None]]
    unnamed x17 -> x9, local copies, waits for them, and re-layouts: 40.1 us -> 7.04 us
    dynamic_slice x96 -> x0, local copies, waits for them, and re-layouts: 23.5 us -> none  [the longest x32 18.6 us: shards(): result = lax.map(conv_rows, starts)]
  transfers between devices with their start and end apart: 4 -> 0, of which waited for: 2 -> 0; matrix products, arithmetic and copies ran while one was open for 1% -> 0% of each run, Pallas kernels for 0% -> 0%
where the time goes in v1:
time: 185 us; the launch traced here: 183 us
  Pallas kernels  170 us (92%)
  local copies, waits for them, and re-layouts  12.1 us (7%)
    pallas_call x1, Pallas kernels, shards(): pl.pallas_call(functools.partial(kernel, nt, nf), out_shape=jax.ShapeDtyp...  170 us
    unnamed x9, local copies, waits for them, and re-layouts  7.04 us

profile of v1, /device:TPU:1, one launch (start us, length us, event | category | flops | bytes accessed | tf_op | source)
XLA Modules:
  0.0 182.7 jit_solution(16515127648914077880)
XLA Ops:
  0.0 1.0 copy.15
  1.0 0.1 reshape.6
  1.2 1.8 copy.14
  3.0 0.1 bitcast_dynamic-update-slice_fusion.6
  3.0 0.1 bitcast_dynamic-update-slice_fusion.5
  3.1 0.1 bitcast_dynamic-update-slice_fusion.4
  3.1 0.1 bitcast_dynamic-update-slice_fusion.3
  3.2 0.1 bitcast_dynamic-update-slice_fusion.2
  3.3 0.1 bitcast_dynamic-update-slice_fusion.1
  3.3 0.1 bitcast_dynamic-update-slice_fusion
  3.4 1.6 copy.16
  5.0 2.3 %reshape.7.bands = bf16[512,960]{1,0:T(8,128)(2,1)} reshape(bf16[64,8,3,320]{3,2,1,0:T(4,128)(2,1)S(1)} %copy.16) | data formatting | bytes 1966080 | tf_op jit(solution)/shard_map/reshape | solution.py:267
  7.3 170.5 %shard_map.55 = bf16[32,64,1024]{2,1,0:T(8,128)(2,1)} custom-call(bf16[512,2048]{1,0:T(8,128)(2,1)} %wave.1, bf16[256,512]{1,0:T(8,128)(2,1)} %bitcast.26, bf16[512,960]{1,0:T(8,128)(2,1)} %reshape.7.bands, s32[1,4096]{1,0:T(1,128)} %bitcast.28, s32[8,128]{1,0:T(8,128)} %bitcast.29), custom_call_target="tpu_custom_call" | custom-call | tf_op jit(solution)/shard_map/pallas_call | solution.py:271
  177.7 4.9 %copy.25 = bf16[1024,32,64]{0,2,1:T(8,128)(2,1)} copy(bf16[1024,32,64]{0,2,1:T(8,128)(2,1)} %bitcast.25) | data formatting | bytes 8388608
  (1 shorter events, 0.0 us)

commit v2 on v1

--- a/solution.py
+++ b/solution.py
@@ -80,19 +80,23 @@
         for g in range(half):
             s[side * half + g, b * blk:(b + 1) * blk, :] = res[g * blk:(g + 1) * blk]
 
+    ahead = 8
     mine = f // half
+    line = [(k, b) for b in range(nb) for p in range(half) for k in (nf - 1 - p, half - 1 - p)]
     for b in range(nb):
         if b == nb - 1:
             @pl.when(t < nt - 1)
             def _():
                 rim_copy(t).wait_recv()
         features(b, 1 - mine)
-        for k in range(nf - 1, half - 1, -1):
-            first(k, b).start()
+        for at, (k, c) in enumerate(line[:ahead]):
+            if c == b and k >= half:
+                first(k, b).start()
     for b in range(nb):
         features(b, mine)
-        for k in range(half - 1, 0, -1):
-            first(k, b).start()
+        for at, (k, c) in enumerate(line[:ahead]):
+            if c == b and 0 < k < half:
+                first(k, b).start()
 
     chans = section.shape[1]
     sec = section[...]
@@ -151,34 +155,35 @@
             src_ref=src, dst_ref=dst, send_sem=h_send.at[k, i, 0 if upper else 1], recv_sem=sem,
             device_id=(to, f), device_id_type=MESH)
 
-    order = list(range(nf - 1, half - 1, -1)), list(range(half - 1, -1, -1))
-    for ks in order:
-        for b in range(nb):
-            for k in ks:
-                if k > 0:
-                    first(k, b).wait_recv()
-                for i in range(nsub):
-                    to, local, remote = second(k, b, i)
-
-                    @pl.when(to == t)
+    sent = [0] * nf
+    for at, (k, b) in enumerate(line):
+        if k > 0:
+            first(k, b).wait_recv()
+        if at + ahead < len(line) and line[at + ahead][0] > 0:
+            first(*line[at + ahead]).start()
+        for i in range(nsub):
+            to, local, remote = second(k, b, i)
+
+            @pl.when(to == t)
+            def _():
+                local.start()
+
+            @pl.when(to != t)
+            def _():
+                remote.start()
+
+            if sent[k] == nb - 1:
+                for upper in (True, False):
+                    there, to, local, remote = halo(k, i, upper)
+
+                    @pl.when(jnp.logical_and(there, to == t))
                     def _():
                         local.start()
 
-                    @pl.when(to != t)
+                    @pl.when(jnp.logical_and(there, to != t))
                     def _():
                         remote.start()
-
-                    if b == nb - 1:
-                        for upper in (True, False):
-                            there, to, local, remote = halo(k, i, upper)
-
-                            @pl.when(jnp.logical_and(there, to == t))
-                            def _():
-                                local.start()
-
-                            @pl.when(jnp.logical_and(there, to != t))
-                            def _():
-                                remote.start()
+        sent[k] += 1
 
     for source in range(nt):
         for slot in range(ndc):

time: 185 us -> 139 us (0.75)
  Pallas kernels: 170 us -> 124 us
    pallas_call x1, Pallas kernels: 170 us -> 124 us  [shards(): pl.pallas_call(functools.partial(kernel, nt, nf), out_shape=jax.ShapeDtyp...]
where the time goes in v2:
time: 139 us; the launch traced here: 137 us
  Pallas kernels  124 us (89%)
  local copies, waits for them, and re-layouts  12.1 us (9%)
    pallas_call x1, Pallas kernels, shards(): pl.pallas_call(functools.partial(kernel, nt, nf), out_shape=jax.ShapeDtyp...  124 us
    unnamed x9, local copies, waits for them, and re-layouts  7.04 us

profile of v2, /device:TPU:1, one launch (start us, length us, event | category | flops | bytes accessed | tf_op | source)
XLA Modules:
  0.0 136.6 jit_solution(2021544464263998338)
XLA Ops:
  0.0 1.0 copy.15
  1.0 0.1 reshape.6
  1.2 1.8 %copy.14 = bf16[512,256]{0,1:T(8,128)(2,1)} copy(bf16[512,256]{1,0:T(8,128)(2,1)} %param.6) | data formatting | bytes 524288 | tf_op args[1]
  3.0 0.1 bitcast_dynamic-update-slice_fusion.6
  3.0 0.1 bitcast_dynamic-update-slice_fusion.5
  3.1 0.1 bitcast_dynamic-update-slice_fusion.4
  3.1 0.1 bitcast_dynamic-update-slice_fusion.3
  3.2 0.1 bitcast_dynamic-update-slice_fusion.2
  3.3 0.1 bitcast_dynamic-update-slice_fusion.1
  3.3 0.1 bitcast_dynamic-update-slice_fusion
  3.4 1.6 %copy.16 = bf16[64,8,3,320]{3,2,1,0:T(4,128)(2,1)S(1)} copy(bf16[64,8,3,320]{0,3,2,1:T(8,128)(2,1)S(1)} %bitcast_dynamic-update-slice_fusion) | data formatting | bytes 1966080 | tf_op jit(solution)/shard_map/stack | solution.py:270
  5.0 2.3 %reshape.7.bands = bf16[512,960]{1,0:T(8,128)(2,1)} reshape(bf16[64,8,3,320]{3,2,1,0:T(4,128)(2,1)S(1)} %copy.16) | data formatting | bytes 1966080 | tf_op jit(solution)/shard_map/reshape | solution.py:272
  7.3 124.4 %shard_map.55 = bf16[32,64,1024]{2,1,0:T(8,128)(2,1)} custom-call(bf16[512,2048]{1,0:T(8,128)(2,1)} %wave.1, bf16[256,512]{1,0:T(8,128)(2,1)} %bitcast.26, bf16[512,960]{1,0:T(8,128)(2,1)} %reshape.7.bands, s32[1,4096]{1,0:T(1,128)} %bitcast.28, s32[8,128]{1,0:T(8,128)} %bitcast.29), custom_call_target="tpu_custom_call" | custom-call | tf_op jit(solution)/shard_map/pallas_call | solution.py:276
  131.7 4.9 %copy.25 = bf16[1024,32,64]{0,2,1:T(8,128)(2,1)} copy(bf16[1024,32,64]{0,2,1:T(8,128)(2,1)} %bitcast.25) | data formatting | bytes 8388608
  (1 shorter events, 0.0 us)
